TPU v7x, 32 devices: a whole 2x2x4 slice. The times are simulated.
32 devices in a mesh: parts: 2 (over y), aper: 4 (over z), rng: 2 (over x), sub: 2 (over core).
Axes of the slice: x: 2, y: 2, z: 4, core: 2. Of those that a mesh axis runs over, the one named last changes fastest.
Arguments:
- echoes: bfloat16 [2, 1024, 2048], P(None, ('parts', 'aper', 'sub'), 'rng'), parts along dimension 1, may hold values from -6 to 6
- chirp: bfloat16 [2, 512], replicated, may hold values from -0.1875 to 0.1875
- pulse_phase: float32 [1024, 64], P(('parts', 'aper', 'sub')), parts along dimension 0, may hold values from -3.140625 to 3.140625
- pulse_shift: int32 [1024, 64], P(('parts', 'aper', 'sub')), parts along dimension 0, may hold values from -8 to 8
- kernel_taps: int32 [2, 2, 8, 512], P(None, None, None, ('parts', 'aper', 'sub')), parts along dimension 3, may hold values from 0 to 31
- merge_shift: int32 [2, 2, 512], P(None, None, ('parts', 'aper', 'sub')), parts along dimension 2, may hold values from -8 to 8
- kernel_weights: float32 [2, 2, 2, 8, 512], P(None, None, None, None, ('parts', 'aper', 'sub')), parts along dimension 4, may hold values from -1 to 1
Outputs:
- image: bfloat16 [2, 512, 2048], P(None, ('parts', 'aper', 'sub'), 'rng'), parts along dimension 1
There are 2 independent parts, one for each index of `parts`. A program takes and returns all parts, laid end to end along the dimension named above; an argument that names none is the same for every part. Nothing has to cross between parts.
All inputs are finite; a program needn't handle non-finite values.
Results may differ from a plain program's by a relative error of at most 0.0099.
Values may be sent and summed in bfloat16 or wider, within the bound.
A program may use at most 128 MiB of HBM per device.

v0:
```python
import functools
import math

import jax
import jax.numpy as jnp
from jax import lax
from jax.experimental import pallas as pl
from jax.experimental.pallas import tpu as pltpu
from jax.sharding import PartitionSpec as P

REACH = 8
EDGE = 128
TILE = 256
MESH = pl.DeviceIdType.MESH
F32 = jnp.float32
BF16 = jnp.bfloat16


def roll_left(value, by):
    width = value.shape[1]
    by = by % width
    return value if by == 0 else pltpu.roll(value, width - by, 1)


def image_kernel(
    n_rng, n_aper, levels, halos,
    echoes, chirp, phase, shift, ktaps, mshift, kweights,
    out,
    cells, filt, phases, shifts, select, pulses, products, image, sibling, kernels, row_shift,
    own_sem, halo_send, halo_recv, sub_send, sub_recv, lev_send, lev_recv,
):
    rng = lax.axis_index("rng")
    aper = lax.axis_index("aper")
    sub = lax.axis_index("sub")
    local, slab = echoes.shape[1], echoes.shape[2]
    n_taps = chirp.shape[1]
    beams = out.shape[1]
    rows = 2 * beams
    width = slab + 2 * EDGE
    window = TILE + n_taps
    offsets = 2 * REACH + 1
    reach_devs = len(halos)

    barrier = pltpu.get_barrier_semaphore()
    pl.semaphore_signal(barrier, inc=1, device_id={"sub": 1 - sub}, device_id_type=MESH)

    def aper_partner(level):
        stride = 2**level
        side = lax.rem(aper // stride, 2)
        return aper + stride - 2 * stride * side, side

    for level in range(levels):
        pl.semaphore_signal(
            barrier, inc=1, device_id={"aper": aper_partner(level)[0]}, device_id_type=MESH
        )
    for dist in range(1, reach_devs + 1):
        @pl.when(rng + dist < n_rng)
        def _():
            pl.semaphore_signal(barrier, inc=1, device_id={"rng": rng + dist}, device_id_type=MESH)

        @pl.when(rng >= dist)
        def _():
            pl.semaphore_signal(barrier, inc=1, device_id={"rng": rng - dist}, device_id_type=MESH)

    own_copy = pltpu.make_async_copy(echoes, cells.at[:, :, pl.ds(EDGE, slab)], own_sem)
    own_copy.start()
    if reach_devs >= n_rng - 1:
        rng_peers = n_rng - 1
    else:
        rng_peers = jnp.minimum(rng, reach_devs) + jnp.minimum(n_rng - 1 - rng, reach_devs)
    pl.semaphore_wait(barrier, 1 + levels + rng_peers)

    def right_copy(index):
        dist = index + 1
        return pltpu.make_async_remote_copy(
            src_ref=echoes.at[:, :, pl.ds(0, halos[index])],
            dst_ref=cells.at[:, :, pl.ds(EDGE + dist * slab, halos[index])],
            send_sem=halo_send.at[index],
            recv_sem=halo_recv.at[index],
            device_id={"rng": rng - dist},
            device_id_type=MESH,
        )

    left_copy = pltpu.make_async_remote_copy(
        src_ref=echoes.at[:, :, pl.ds(slab - EDGE, EDGE)],
        dst_ref=cells.at[:, :, pl.ds(0, EDGE)],
        send_sem=halo_send.at[reach_devs],
        recv_sem=halo_recv.at[reach_devs],
        device_id={"rng": rng + 1},
        device_id_type=MESH,
    )
    for index in range(reach_devs):
        @pl.when(rng >= index + 1)
        def _():
            right_copy(index).start()

        @pl.when(rng + index + 1 >= n_rng)
        def _():
            cells[:, :, EDGE + (index + 1) * slab : EDGE + (index + 1) * slab + halos[index]] = (
                jnp.zeros((2, local, halos[index]), BF16)
            )

    @pl.when(rng + 1 < n_rng)
    def _():
        left_copy.start()

    @pl.when(rng == 0)
    def _():
        cells[:, :, 0:EDGE] = jnp.zeros((2, local, EDGE), BF16)

    def sub_copy(src, dst, index):
        return pltpu.make_async_remote_copy(
            src_ref=src,
            dst_ref=dst,
            send_sem=sub_send.at[index],
            recv_sem=sub_recv.at[index],
            device_id={"sub": 1 - sub},
            device_id_type=MESH,
        )

    phase_copy = sub_copy(phase, phases, 0)
    shift_copy = sub_copy(shift, shifts, 1)
    phase_copy.start()
    shift_copy.start()

    taps_row = jnp.concatenate(
        [chirp[...].astype(F32), jnp.zeros((2, window - n_taps), F32)], axis=1
    )
    for part in range(2):
        spread = jnp.broadcast_to(taps_row[part : part + 1, :], (TILE, window))
        filt[part * TILE : (part + 1) * TILE, :] = pltpu.roll(
            spread, 0, 1, stride=1, stride_axis=0
        ).astype(BF16)

    beam_ids = lax.broadcasted_iota(jnp.int32, (beams, rows), 0)
    for level in range(levels):
        for child in range(2):
            tap = ktaps[level, child]
            real_w, imag_w = kweights[0, level, child], kweights[1, level, child]
            tap2 = jnp.concatenate([tap, tap], axis=1)
            upper_w = jnp.concatenate([real_w, imag_w], axis=1)
            lower_w = jnp.concatenate([-imag_w, real_w], axis=1)
            upper = jnp.zeros((beams, rows), F32)
            lower = jnp.zeros((beams, rows), F32)
            for t in range(tap.shape[0]):
                match = beam_ids == tap2[t : t + 1, :]
                upper = upper + jnp.where(match, upper_w[t : t + 1, :], 0.0)
                lower = lower + jnp.where(match, lower_w[t : t + 1, :], 0.0)
            kernels[level, child] = jnp.concatenate([upper, lower], axis=0).T.astype(BF16)
            row = mshift[level, child : child + 1, :]
            row2 = jnp.concatenate([row, row], axis=1) + REACH
            row_shift[level, child] = jnp.broadcast_to(row2, (rows, rows)).T

    phase_copy.wait()
    shift_copy.wait()

    def own_beams(own, got):
        stacked = jnp.concatenate([own, own, got, got], axis=0).T
        return jnp.where(sub == 0, stacked[:beams], stacked[beams:])

    angle = own_beams(phase[...], phases[...])
    lag = own_beams(shift[...], shifts[...])
    scale = 1.0 / math.sqrt(2 * local)
    cosine, sine = jnp.cos(angle) * scale, jnp.sin(angle) * scale
    is_real = lax.rem(lax.broadcasted_iota(jnp.int32, (beams, 4 * local), 1), 2 * local) < local
    upper = jnp.where(is_real, cosine, -sine)
    lower = jnp.where(is_real, sine, cosine)
    for index in range(offsets):
        match = lag == index - REACH
        select[index * rows : index * rows + beams, :] = jnp.where(match, upper, 0.0).astype(BF16)
        select[index * rows + beams : (index + 1) * rows, :] = jnp.where(
            match, lower, 0.0
        ).astype(BF16)

    own_copy.wait()

    @pl.when(rng > 0)
    def _():
        left_copy.wait_recv()

    for index in range(reach_devs):
        @pl.when(rng + index + 1 < n_rng)
        def _():
            right_copy(index).wait_recv()

    def valid(first, columns):
        bins = lax.broadcasted_iota(jnp.int32, (8, columns), 1) + (first - EDGE) + rng * slab
        return ((bins >= 0) & (bins < n_rng * slab))[0:1]

    for tile in range(width // TILE):
        first = tile * TILE
        data = cells[:, :, first : first + window].reshape(2 * local, window)
        both = lax.dot_general(
            data, filt[...], (((1,), (1,)), ((), ())), preferred_element_type=F32
        )
        keep = valid(first, TILE)
        real = both[:local, :TILE] + both[local:, TILE:]
        imag = both[local:, :TILE] - both[:local, TILE:]
        pulses[0, 0, :, first : first + TILE] = jnp.where(keep, real, 0.0).astype(BF16)
        pulses[0, 1, :, first : first + TILE] = jnp.where(keep, imag, 0.0).astype(BF16)

    pulse_copy = sub_copy(pulses.at[0], pulses.at[1], 2)
    pulse_copy.start()
    pulse_copy.wait()

    for tile in range(width // TILE):
        first = tile * TILE
        block = pulses[:, :, :, first : first + TILE].reshape(4 * local, TILE)
        products[:, first : first + TILE] = jnp.dot(
            select[...], block, preferred_element_type=F32
        )

    chunk = 16
    chunks = rows // chunk
    keep_all = valid(0, width)

    def level_copy(level, piece):
        return pltpu.make_async_remote_copy(
            src_ref=image.at[level, pl.ds(piece * chunk, chunk)],
            dst_ref=sibling.at[level, pl.ds(piece * chunk, chunk)],
            send_sem=lev_send.at[level * chunks + piece],
            recv_sem=lev_recv.at[level * chunks + piece],
            device_id={"aper": aper_partner(level)[0]},
            device_id_type=MESH,
        )

    for piece in range(chunks):
        for half in range(2):
            at = piece * chunk + half * 8
            total = jnp.zeros((8, width), F32)
            for index in range(offsets):
                part = products[index * rows + at : index * rows + at + 8, :]
                total = total + roll_left(part, index - REACH)
            products[at : at + 8, :] = jnp.where(keep_all, total, 0.0)
        image[0, piece * chunk : (piece + 1) * chunk, :] = products[
            piece * chunk : (piece + 1) * chunk, :
        ].astype(BF16)
        level_copy(0, piece).start()

    def moved(level, child_of, source):
        matrix = jnp.where(child_of == 0, kernels[level, 0], kernels[level, 1])
        by = jnp.where(child_of == 0, row_shift[level, 0], row_shift[level, 1])
        value = jnp.dot(matrix, source, preferred_element_type=F32)
        out_rows = []
        for first in range(0, rows, 8):
            part = value[first : first + 8]
            lanes = by[first : first + 8, 0:1]
            bit = 1
            while bit <= 2 * REACH:
                part = jnp.where((lanes & bit) != 0, roll_left(part, bit), part)
                bit *= 2
            out_rows.append(part)
        return out_rows

    for level in range(levels):
        side = aper_partner(level)[1]
        own = moved(level, side, image[level])
        for first in range(0, rows, 8):
            products[first : first + 8, :] = own[first // 8]
        for piece in range(chunks):
            level_copy(level, piece).wait_recv()
        other = moved(level, 1 - side, sibling[level])
        for piece in range(chunks):
            at = piece * chunk
            merged = jnp.concatenate(
                [
                    jnp.where(
                        keep_all,
                        roll_left(products[a : a + 8, :] + other[a // 8], -REACH),
                        0.0,
                    )
                    for a in (at, at + 8)
                ],
                axis=0,
            ).astype(BF16)
            if level < levels - 1:
                image[level + 1, at : at + chunk, :] = merged
                level_copy(level + 1, piece).start()
            else:
                out[at // beams, at % beams : at % beams + chunk, :] = merged[
                    :, EDGE : EDGE + slab
                ]

    pl_levels = range(levels)
    for level in pl_levels:
        for piece in range(chunks):
            level_copy(level, piece).wait_send()
    for index in range(reach_devs):
        @pl.when(rng >= index + 1)
        def _():
            right_copy(index).wait_send()

    @pl.when(rng + 1 < n_rng)
    def _():
        left_copy.wait_send()


def shards(n_rng, n_aper, echoes, chirp, phase, shift, ktaps, mshift, kweights):
    local, slab = echoes.shape[1], echoes.shape[2]
    n_taps = chirp.shape[1]
    beams = ktaps.shape[3]
    rows = 2 * beams
    levels = n_aper.bit_length() - 1
    width = slab + 2 * EDGE
    need = n_taps + EDGE
    halos = []
    while need > 0:
        halos.append(min(slab, need))
        need -= slab
    halo = n_taps + EDGE
    offsets = 2 * REACH + 1
    pieces = levels * (rows // 16)
    vmem = pl.BlockSpec(memory_space=pltpu.VMEM)
    return pl.pallas_call(
        functools.partial(image_kernel, n_rng, n_aper, levels, tuple(halos)),
        out_shape=jax.ShapeDtypeStruct((2, beams, slab), BF16),
        in_specs=[pl.BlockSpec(memory_space=pl.ANY)] + [vmem] * 6,
        out_specs=vmem,
        scratch_shapes=[
            pltpu.VMEM((2, local, EDGE + slab + halo), BF16),
            pltpu.VMEM((2 * TILE, TILE + n_taps), BF16),
            pltpu.VMEM(phase.shape, F32),
            pltpu.VMEM(shift.shape, jnp.int32),
            pltpu.VMEM((offsets * rows, 4 * local), BF16),
            pltpu.VMEM((2, 2, local, width), BF16),
            pltpu.VMEM((offsets * rows, width), F32),
            pltpu.VMEM((levels, rows, width), BF16),
            pltpu.VMEM((levels, rows, width), BF16),
            pltpu.VMEM((levels, 2, rows, rows), BF16),
            pltpu.VMEM((levels, 2, rows, rows), jnp.int32),
            pltpu.SemaphoreType.DMA,
            pltpu.SemaphoreType.DMA((len(halos) + 1,)),
            pltpu.SemaphoreType.DMA((len(halos) + 1,)),
            pltpu.SemaphoreType.DMA((3,)),
            pltpu.SemaphoreType.DMA((3,)),
            pltpu.SemaphoreType.DMA((pieces,)),
            pltpu.SemaphoreType.DMA((pieces,)),
        ],
        compiler_params=pltpu.CompilerParams(
            collective_id=0, has_side_effects=True, vmem_limit_bytes=40 * 2**20
        ),
    )(echoes, chirp, phase, shift, ktaps, mshift, kweights)


def solution(mesh):
    placed = (
        P(None, ("parts", "aper", "sub"), "rng"),
        P(),
        P(("parts", "aper", "sub"), None),
        P(("parts", "aper", "sub"), None),
        P(None, None, None, ("parts", "aper", "sub")),
        P(None, None, ("parts", "aper", "sub")),
        P(None, None, None, None, ("parts", "aper", "sub")),
    )
    return jax.shard_map(
        functools.partial(shards, mesh.shape["rng"], mesh.shape["aper"]),
        mesh=mesh,
        in_specs=placed,
        out_specs=P(None, ("parts", "aper", "sub"), "rng"),
        check_vma=False,
    )
```

profile of v0, /device:TPU:0, one launch (start us, length us, event | category | flops | bytes accessed | tf_op | source)
XLA Modules:
  0.0 36.4 jit_solution(15399706347112630693)
XLA Ops:
  0.0 0.0 copy-start
  0.0 0.9 %copy-done = bf16[2,64,1024]{2,1,0:T(8,128)(2,1)S(1)} copy-done((bf16[2,64,1024]{2,1,0:T(8,128)(2,1)S(1)}, bf16[2,64,1024]{2,1,0:T(8,128)(2,1)}, u32[]{:S(2)}) %copy-start) | copy-done | bytes 262168
  1.0 0.0 copy-start.1
  1.0 0.8 %copy-done.1 = f32[64,64]{1,0:T(8,128)S(1)} copy-done((f32[64,64]{1,0:T(8,128)S(1)}, f32[64,64]{1,0:T(8,128)}, u32[]{:S(2)}) %copy-start.1) | copy-done | bytes 16408
  1.7 0.0 copy-start.2
  1.7 0.8 %copy-done.2 = s32[64,64]{1,0:T(8,128)S(1)} copy-done((s32[64,64]{1,0:T(8,128)S(1)}, s32[64,64]{1,0:T(8,128)}, u32[]{:S(2)}) %copy-start.2) | copy-done | bytes 16408
  2.5 0.0 copy-start.3
  2.5 0.8 %copy-done.3 = f32[2,2,2,8,32]{4,3,2,1,0:T(8,128)S(1)} copy-done((f32[2,2,2,8,32]{4,3,2,1,0:T(8,128)S(1)}, f32[2,2,2,8,32]{4,3,2,1,0:T(8,128)}, u32[]{:S(2)}) %copy-start.3) | copy-done | bytes 8216
  3.2 0.0 copy-start.4
  3.2 0.7 %copy-done.4 = s32[2,2,8,32]{3,2,1,0:T(8,128)S(1)} copy-done((s32[2,2,8,32]{3,2,1,0:T(8,128)S(1)}, s32[2,2,8,32]{3,2,1,0:T(8,128)}, u32[]{:S(2)}) %copy-start.4) | copy-done | bytes 4120
  3.9 0.0 copy-start.5
  3.9 0.7 %copy-done.5 = bf16[2,512]{1,0:T(2,128)(2,1)S(1)} copy-done((bf16[2,512]{1,0:T(2,128)(2,1)S(1)}, bf16[2,512]{1,0:T(2,128)(2,1)}, u32[]{:S(2)}) %copy-start.5) | copy-done | bytes 2072
  4.6 0.0 copy-start.6
  4.6 0.7 %copy-done.6 = s32[2,2,32]{2,1,0:T(2,128)S(1)} copy-done((s32[2,2,32]{2,1,0:T(2,128)S(1)}, s32[2,2,32]{2,1,0:T(2,128)}, u32[]{:S(2)}) %copy-start.6) | copy-done | bytes 536
  5.3 30.4 %shard_map.73 = bf16[2,32,1024]{2,1,0:T(8,128)(2,1)S(1)} custom-call(bf16[2,64,1024]{2,1,0:T(8,128)(2,1)S(1)} %copy-done, bf16[2,512]{1,0:T(2,128)(2,1)S(1)} %copy-done.5, f32[64,64]{1,0:T(8,128)S(1)} %copy-done.1, s32[64,64]{1,0:T(8,128)S(1)} %copy-done.2, s32[2,2,8,32]{3,2,1,0:T(8,128)S(1)} %copy-done.4, s32[2,2,32]{2,1,0:T(2,128)S(1)} %copy-done.6, ...), custom_call_target="tpu_custom_call" | custom-call | tf_op jit(solution)/shard_map/pallas_call | solution.py:314
  35.7 0.7 %copy.9 = bf16[2,32,1024]{2,1,0:T(8,128)(2,1)} copy(bf16[2,32,1024]{2,1,0:T(8,128)(2,1)S(1)} %shard_map.73) | data formatting | bytes 262144
Async XLA Ops:
  0.0 0.9 %copy-start = (bf16[2,64,1024]{2,1,0:T(8,128)(2,1)S(1)}, bf16[2,64,1024]{2,1,0:T(8,128)(2,1)}, u32[]{:S(2)}) copy-start(bf16[2,64,1024]{2,1,0:T(8,128)(2,1)} %echoes.1) | copy-start | bytes 786436
  1.0 0.8 %copy-start.1 = (f32[64,64]{1,0:T(8,128)S(1)}, f32[64,64]{1,0:T(8,128)}, u32[]{:S(2)}) copy-start(f32[64,64]{1,0:T(8,128)} %phase.1) | copy-start | bytes 49156
  1.7 0.8 %copy-start.2 = (s32[64,64]{1,0:T(8,128)S(1)}, s32[64,64]{1,0:T(8,128)}, u32[]{:S(2)}) copy-start(s32[64,64]{1,0:T(8,128)} %shift.1) | copy-start | bytes 49156
  2.5 0.8 %copy-start.3 = (f32[2,2,2,8,32]{4,3,2,1,0:T(8,128)S(1)}, f32[2,2,2,8,32]{4,3,2,1,0:T(8,128)}, u32[]{:S(2)}) copy-start(f32[2,2,2,8,32]{4,3,2,1,0:T(8,128)} %kweights.1) | copy-start | bytes 24580
  3.2 0.7 %copy-start.4 = (s32[2,2,8,32]{3,2,1,0:T(8,128)S(1)}, s32[2,2,8,32]{3,2,1,0:T(8,128)}, u32[]{:S(2)}) copy-start(s32[2,2,8,32]{3,2,1,0:T(8,128)} %ktaps.1) | copy-start | bytes 12292
  3.9 0.7 %copy-start.5 = (bf16[2,512]{1,0:T(2,128)(2,1)S(1)}, bf16[2,512]{1,0:T(2,128)(2,1)}, u32[]{:S(2)}) copy-start(bf16[2,512]{1,0:T(2,128)(2,1)} %chirp.1) | copy-start | bytes 6148
  4.6 0.7 %copy-start.6 = (s32[2,2,32]{2,1,0:T(2,128)S(1)}, s32[2,2,32]{2,1,0:T(2,128)}, u32[]{:S(2)}) copy-start(s32[2,2,32]{2,1,0:T(2,128)} %mshift.1) | copy-start | bytes 1540
where the time goes:
time: 36.8 us; the launch traced here: 36.4 us
  Pallas kernels  30.4 us (83%)
  local copies, waits for them, and re-layouts  5.96 us (16%)
    pallas_call x1, Pallas kernels, shards(): pl.pallas_call(functools.partial(image_kernel, n_rng, n_aper, levels, tup...  30.4 us
    unnamed x15, local copies, waits for them, and re-layouts  5.96 us

commit v1 on v0

--- a/solution.py
+++ b/solution.py
@@ -10,6 +10,7 @@
 
 REACH = 8
 EDGE = 128
+HALF = EDGE // 2
 TILE = 256
 MESH = pl.DeviceIdType.MESH
 F32 = jnp.float32
@@ -24,9 +25,9 @@
 
 def image_kernel(
     n_rng, n_aper, levels, halos,
-    echoes, chirp, phase, shift, ktaps, mshift, kweights,
+    echoes, chirp, phase_in, shift_in, ktaps_in, mshift_in, kweights_in,
     out,
-    cells, filt, phases, shifts, select, pulses, products, image, sibling, kernels, row_shift,
+    phase, shift, ktaps, mshift, kweights, cells, filt, phases, shifts, select, pulses, products, image, sibling, kernels, row_shift,
     own_sem, halo_send, halo_recv, sub_send, sub_recv, lev_send, lev_recv,
 ):
     rng = lax.axis_index("rng")
@@ -39,7 +40,9 @@
     width = slab + 2 * EDGE
     window = TILE + n_taps
     offsets = 2 * REACH + 1
-    reach_devs = len(halos)
+    reach_devs = halos[-1][0]
+    circle = slab + EDGE
+    left_index = len(halos)
 
     barrier = pltpu.get_barrier_semaphore()
     pl.semaphore_signal(barrier, inc=1, device_id={"sub": 1 - sub}, device_id_type=MESH)
@@ -62,8 +65,15 @@
         def _():
             pl.semaphore_signal(barrier, inc=1, device_id={"rng": rng - dist}, device_id_type=MESH)
 
-    own_copy = pltpu.make_async_copy(echoes, cells.at[:, :, pl.ds(EDGE, slab)], own_sem)
+    own_copy = pltpu.make_async_copy(echoes, cells.at[:, :, pl.ds(EDGE, slab)], own_sem.at[0])
     own_copy.start()
+    tables = ((phase_in, phase), (shift_in, shift), (ktaps_in, ktaps), (mshift_in, mshift),
+              (kweights_in, kweights))
+    loads = [
+        pltpu.make_async_copy(src, dst, own_sem.at[1 + i]) for i, (src, dst) in enumerate(tables)
+    ]
+    for load in loads:
+        load.start()
     if reach_devs >= n_rng - 1:
         rng_peers = n_rng - 1
     else:
@@ -71,10 +81,10 @@
     pl.semaphore_wait(barrier, 1 + levels + rng_peers)
 
     def right_copy(index):
-        dist = index + 1
+        dist, start, count = halos[index]
         return pltpu.make_async_remote_copy(
-            src_ref=echoes.at[:, :, pl.ds(0, halos[index])],
-            dst_ref=cells.at[:, :, pl.ds(EDGE + dist * slab, halos[index])],
+            src_ref=echoes.at[:, :, pl.ds(start, count)],
+            dst_ref=cells.at[:, :, pl.ds(EDGE + dist * slab + start, count)],
             send_sem=halo_send.at[index],
             recv_sem=halo_recv.at[index],
             device_id={"rng": rng - dist},
@@ -84,21 +94,20 @@
     left_copy = pltpu.make_async_remote_copy(
         src_ref=echoes.at[:, :, pl.ds(slab - EDGE, EDGE)],
         dst_ref=cells.at[:, :, pl.ds(0, EDGE)],
-        send_sem=halo_send.at[reach_devs],
-        recv_sem=halo_recv.at[reach_devs],
+        send_sem=halo_send.at[left_index],
+        recv_sem=halo_recv.at[left_index],
         device_id={"rng": rng + 1},
         device_id_type=MESH,
     )
-    for index in range(reach_devs):
-        @pl.when(rng >= index + 1)
+    for index, (dist, start, count) in enumerate(halos):
+        @pl.when(rng >= dist)
         def _():
             right_copy(index).start()
 
-        @pl.when(rng + index + 1 >= n_rng)
+        @pl.when(rng + dist >= n_rng)
         def _():
-            cells[:, :, EDGE + (index + 1) * slab : EDGE + (index + 1) * slab + halos[index]] = (
-                jnp.zeros((2, local, halos[index]), BF16)
-            )
+            first = EDGE + dist * slab + start
+            cells[:, :, first : first + count] = jnp.zeros((2, local, count), BF16)
 
     @pl.when(rng + 1 < n_rng)
     def _():
@@ -118,8 +127,8 @@
             device_id_type=MESH,
         )
 
-    phase_copy = sub_copy(phase, phases, 0)
-    shift_copy = sub_copy(shift, shifts, 1)
+    phase_copy = sub_copy(phase_in, phases, 0)
+    shift_copy = sub_copy(shift_in, shifts, 1)
     phase_copy.start()
     shift_copy.start()
 
@@ -131,6 +140,9 @@
         filt[part * TILE : (part + 1) * TILE, :] = pltpu.roll(
             spread, 0, 1, stride=1, stride_axis=0
         ).astype(BF16)
+
+    for load in loads:
+        load.wait()
 
     beam_ids = lax.broadcasted_iota(jnp.int32, (beams, rows), 0)
     for level in range(levels):
@@ -174,21 +186,35 @@
 
     own_copy.wait()
 
-    @pl.when(rng > 0)
-    def _():
-        left_copy.wait_recv()
-
-    for index in range(reach_devs):
-        @pl.when(rng + index + 1 < n_rng)
-        def _():
-            right_copy(index).wait_recv()
-
     def valid(first, columns):
         bins = lax.broadcasted_iota(jnp.int32, (8, columns), 1) + (first - EDGE) + rng * slab
         return ((bins >= 0) & (bins < n_rng * slab))[0:1]
 
-    for tile in range(width // TILE):
+    tiles = width // TILE
+    order = list(range(1, tiles))
+    order.insert(1, 0)
+
+    def pulse_copy(tile):
+        at = pl.ds(tile * TILE, TILE)
+        return sub_copy(pulses.at[0, :, :, at], pulses.at[1, :, :, at], 2 + tile)
+
+    arrived = 0
+    for tile in order:
         first = tile * TILE
+        if tile == 0:
+            @pl.when(rng > 0)
+            def _():
+                left_copy.wait_recv()
+        while arrived < len(halos):
+            dist, start, count = halos[arrived]
+            if EDGE + dist * slab + start >= first + window:
+                break
+
+            @pl.when(rng + dist < n_rng)
+            def _():
+                right_copy(arrived).wait_recv()
+
+            arrived += 1
         data = cells[:, :, first : first + window].reshape(2 * local, window)
         both = lax.dot_general(
             data, filt[...], (((1,), (1,)), ((), ())), preferred_element_type=F32
@@ -198,13 +224,11 @@
         imag = both[local:, :TILE] - both[:local, TILE:]
         pulses[0, 0, :, first : first + TILE] = jnp.where(keep, real, 0.0).astype(BF16)
         pulses[0, 1, :, first : first + TILE] = jnp.where(keep, imag, 0.0).astype(BF16)
-
-    pulse_copy = sub_copy(pulses.at[0], pulses.at[1], 2)
-    pulse_copy.start()
-    pulse_copy.wait()
-
-    for tile in range(width // TILE):
+        pulse_copy(tile).start()
+
+    for tile in order:
         first = tile * TILE
+        pulse_copy(tile).wait_recv()
         block = pulses[:, :, :, first : first + TILE].reshape(4 * local, TILE)
         products[:, first : first + TILE] = jnp.dot(
             select[...], block, preferred_element_type=F32
@@ -212,7 +236,10 @@
 
     chunk = 16
     chunks = rows // chunk
-    keep_all = valid(0, width)
+    column = lax.broadcasted_iota(jnp.int32, (8, circle), 1)
+    bins = jnp.where(column < slab + HALF, column, column - circle) + rng * slab
+    keep_all = ((bins >= 0) & (bins < n_rng * slab))[0:1]
+    is_next = lax.broadcasted_iota(jnp.int32, (8, EDGE), 1) < HALF
 
     def level_copy(level, piece):
         return pltpu.make_async_remote_copy(
@@ -227,13 +254,21 @@
     for piece in range(chunks):
         for half in range(2):
             at = piece * chunk + half * 8
-            total = jnp.zeros((8, width), F32)
+            total = jnp.zeros((8, circle), F32)
             for index in range(offsets):
-                part = products[index * rows + at : index * rows + at + 8, :]
+                here = index * rows + at
+                margin = jnp.where(
+                    is_next,
+                    products[here : here + 8, EDGE + slab :],
+                    products[here : here + 8, :EDGE],
+                )
+                part = jnp.concatenate(
+                    [products[here : here + 8, EDGE : EDGE + slab], margin], axis=1
+                )
                 total = total + roll_left(part, index - REACH)
-            products[at : at + 8, :] = jnp.where(keep_all, total, 0.0)
+            products[at : at + 8, :circle] = jnp.where(keep_all, total, 0.0)
         image[0, piece * chunk : (piece + 1) * chunk, :] = products[
-            piece * chunk : (piece + 1) * chunk, :
+            piece * chunk : (piece + 1) * chunk, :circle
         ].astype(BF16)
         level_copy(0, piece).start()
 
@@ -256,7 +291,7 @@
         side = aper_partner(level)[1]
         own = moved(level, side, image[level])
         for first in range(0, rows, 8):
-            products[first : first + 8, :] = own[first // 8]
+            products[first : first + 8, :circle] = own[first // 8]
         for piece in range(chunks):
             level_copy(level, piece).wait_recv()
         other = moved(level, 1 - side, sibling[level])
@@ -266,7 +301,7 @@
                 [
                     jnp.where(
                         keep_all,
-                        roll_left(products[a : a + 8, :] + other[a // 8], -REACH),
+                        roll_left(products[a : a + 8, :circle] + other[a // 8], -REACH),
                         0.0,
                     )
                     for a in (at, at + 8)
@@ -278,15 +313,17 @@
                 level_copy(level + 1, piece).start()
             else:
                 out[at // beams, at % beams : at % beams + chunk, :] = merged[
-                    :, EDGE : EDGE + slab
+                    :, :slab
                 ]
 
     pl_levels = range(levels)
     for level in pl_levels:
         for piece in range(chunks):
             level_copy(level, piece).wait_send()
-    for index in range(reach_devs):
-        @pl.when(rng >= index + 1)
+    for tile in order:
+        pulse_copy(tile).wait_send()
+    for index, (dist, _, _) in enumerate(halos):
+        @pl.when(rng >= dist)
         def _():
             right_copy(index).wait_send()
 
@@ -302,21 +339,25 @@
     rows = 2 * beams
     levels = n_aper.bit_length() - 1
     width = slab + 2 * EDGE
-    need = n_taps + EDGE
     halos = []
-    while need > 0:
-        halos.append(min(slab, need))
-        need -= slab
+    at = 0
+    while at < n_taps + EDGE:
+        ends = ((at + EDGE) // TILE * TILE + EDGE, (at // slab + 1) * slab, n_taps + EDGE)
+        end = min(e for e in ends if e > at)
+        halos.append((at // slab + 1, at % slab, end - at))
+        at = end
     halo = n_taps + EDGE
     offsets = 2 * REACH + 1
     pieces = levels * (rows // 16)
     vmem = pl.BlockSpec(memory_space=pltpu.VMEM)
+    hbm = pl.BlockSpec(memory_space=pltpu.HBM)
+    tables = (phase, shift, ktaps, mshift, kweights)
     return pl.pallas_call(
         functools.partial(image_kernel, n_rng, n_aper, levels, tuple(halos)),
         out_shape=jax.ShapeDtypeStruct((2, beams, slab), BF16),
-        in_specs=[pl.BlockSpec(memory_space=pl.ANY)] + [vmem] * 6,
+        in_specs=[hbm, vmem] + [hbm] * 5,
         out_specs=vmem,
-        scratch_shapes=[
+        scratch_shapes=[pltpu.VMEM(t.shape, t.dtype) for t in tables] + [
             pltpu.VMEM((2, local, EDGE + slab + halo), BF16),
             pltpu.VMEM((2 * TILE, TILE + n_taps), BF16),
             pltpu.VMEM(phase.shape, F32),
@@ -324,20 +365,20 @@
             pltpu.VMEM((offsets * rows, 4 * local), BF16),
             pltpu.VMEM((2, 2, local, width), BF16),
             pltpu.VMEM((offsets * rows, width), F32),
-            pltpu.VMEM((levels, rows, width), BF16),
-            pltpu.VMEM((levels, rows, width), BF16),
+            pltpu.VMEM((levels, rows, slab + EDGE), BF16),
+            pltpu.VMEM((levels, rows, slab + EDGE), BF16),
             pltpu.VMEM((levels, 2, rows, rows), BF16),
             pltpu.VMEM((levels, 2, rows, rows), jnp.int32),
-            pltpu.SemaphoreType.DMA,
+            pltpu.SemaphoreType.DMA((6,)),
             pltpu.SemaphoreType.DMA((len(halos) + 1,)),
             pltpu.SemaphoreType.DMA((len(halos) + 1,)),
-            pltpu.SemaphoreType.DMA((3,)),
-            pltpu.SemaphoreType.DMA((3,)),
+            pltpu.SemaphoreType.DMA((2 + width // TILE,)),
+            pltpu.SemaphoreType.DMA((2 + width // TILE,)),
             pltpu.SemaphoreType.DMA((pieces,)),
             pltpu.SemaphoreType.DMA((pieces,)),
         ],
         compiler_params=pltpu.CompilerParams(
-            collective_id=0, has_side_effects=True, vmem_limit_bytes=40 * 2**20
+            collective_id=0, has_side_effects=True, vmem_limit_bytes=64 * 2**20 - 2**17
         ),
     )(echoes, chirp, phase, shift, ktaps, mshift, kweights)
 

time: 36.8 us -> 29.4 us (0.80)
  local copies, waits for them, and re-layouts: 5.96 us -> 1.57 us
  Pallas kernels: 30.4 us -> 27.7 us
    unnamed x15 -> x1, local copies, waits for them, and re-layouts: 5.96 us -> 1.57 us
    pallas_call x1, Pallas kernels: 30.4 us -> 27.7 us  [shards(): pl.pallas_call(functools.partial(image_kernel, n_rng, n_aper, levels, tup...]
where the time goes in v1:
time: 29.4 us; the launch traced here: 29.3 us
  Pallas kernels  27.7 us (94%)
  local copies, waits for them, and re-layouts  1.57 us (5%)
    pallas_call x1, Pallas kernels, shards(): pl.pallas_call(functools.partial(image_kernel, n_rng, n_aper, levels, tup...  27.7 us
    unnamed x1, local copies, waits for them, and re-layouts  1.57 us

profile of v1, /device:TPU:0, one launch (start us, length us, event | category | flops | bytes accessed | tf_op | source)
XLA Modules:
  0.0 29.3 jit_solution(2176689554412932356)
XLA Ops:
  0.0 27.7 %shard_map.73 = bf16[2,32,1024]{2,1,0:T(8,128)(2,1)} custom-call(bf16[2,64,1024]{2,1,0:T(8,128)(2,1)} %echoes.1, bf16[2,512]{1,0:T(2,128)(2,1)} %chirp.1, f32[64,64]{1,0:T(8,128)} %phase_in.1, s32[64,64]{1,0:T(8,128)} %shift_in.1, s32[2,2,8,32]{3,2,1,0:T(8,128)} %ktaps_in.1, s32[2,2,32]{2,1,0:T(2,128)} %mshift_in.1, f32[2,2,2,8,32]{4,3,2,1,0:T(8,128)} %kweights_in.1), custom_call_target="tpu_custom_call" | custom-call | tf_op jit(solution)/shard_map/pallas_call | solution.py:355
  27.7 1.6 %copy.9 = bf16[2,32,1024]{2,1,0:T(8,128)(2,1)} copy(bf16[2,32,1024]{2,1,0:T(8,128)(2,1)} %shard_map.73) | data formatting | bytes 262144

commit v2 on v1

--- a/solution.py
+++ b/solution.py
@@ -40,6 +40,8 @@
     width = slab + 2 * EDGE
     window = TILE + n_taps
     offsets = 2 * REACH + 1
+    chunk = 16
+    chunks = rows // chunk
     reach_devs = halos[-1][0]
     circle = slab + EDGE
     left_index = len(halos)
@@ -179,10 +181,12 @@
     lower = jnp.where(is_real, sine, cosine)
     for index in range(offsets):
         match = lag == index - REACH
-        select[index * rows : index * rows + beams, :] = jnp.where(match, upper, 0.0).astype(BF16)
-        select[index * rows + beams : (index + 1) * rows, :] = jnp.where(
-            match, lower, 0.0
+        both = jnp.concatenate(
+            [jnp.where(match, upper, 0.0), jnp.where(match, lower, 0.0)], axis=0
         ).astype(BF16)
+        for piece in range(chunks):
+            here = (piece * offsets + index) * chunk
+            select[here : here + chunk, :] = both[piece * chunk : (piece + 1) * chunk]
 
     own_copy.wait()
 
@@ -226,16 +230,6 @@
         pulses[0, 1, :, first : first + TILE] = jnp.where(keep, imag, 0.0).astype(BF16)
         pulse_copy(tile).start()
 
-    for tile in order:
-        first = tile * TILE
-        pulse_copy(tile).wait_recv()
-        block = pulses[:, :, :, first : first + TILE].reshape(4 * local, TILE)
-        products[:, first : first + TILE] = jnp.dot(
-            select[...], block, preferred_element_type=F32
-        )
-
-    chunk = 16
-    chunks = rows // chunk
     column = lax.broadcasted_iota(jnp.int32, (8, circle), 1)
     bins = jnp.where(column < slab + HALF, column, column - circle) + rng * slab
     keep_all = ((bins >= 0) & (bins < n_rng * slab))[0:1]
@@ -252,11 +246,20 @@
         )
 
     for piece in range(chunks):
+        group = slice(piece * offsets * chunk, (piece + 1) * offsets * chunk)
+        for tile in order:
+            first = tile * TILE
+            if piece == 0:
+                pulse_copy(tile).wait_recv()
+            block = pulses[:, :, :, first : first + TILE].reshape(4 * local, TILE)
+            products[group, first : first + TILE] = jnp.dot(
+                select[group, :], block, preferred_element_type=F32
+            )
         for half in range(2):
             at = piece * chunk + half * 8
             total = jnp.zeros((8, circle), F32)
             for index in range(offsets):
-                here = index * rows + at
+                here = (piece * offsets + index) * chunk + half * 8
                 margin = jnp.where(
                     is_next,
                     products[here : here + 8, EDGE + slab :],

time: 29.4 us -> 30.2 us (1.027)
  Pallas kernels: 27.7 us -> 28.5 us
    pallas_call x1, Pallas kernels: 27.7 us -> 28.5 us  [shards(): pl.pallas_call(functools.partial(image_kernel, n_rng, n_aper, levels, tup...]
where the time goes in v2:
time: 30.2 us; the launch traced here: 30.1 us
  Pallas kernels  28.5 us (94%)
  local copies, waits for them, and re-layouts  1.57 us (5%)
    pallas_call x1, Pallas kernels, shards(): pl.pallas_call(functools.partial(image_kernel, n_rng, n_aper, levels, tup...  28.5 us
    unnamed x1, local copies, waits for them, and re-layouts  1.57 us

profile of v2, /device:TPU:0, one launch (start us, length us, event | category | flops | bytes accessed | tf_op | source)
XLA Modules:
  0.0 30.1 jit_solution(1987819126666537551)
XLA Ops:
  0.0 28.5 %shard_map.73 = bf16[2,32,1024]{2,1,0:T(8,128)(2,1)} custom-call(bf16[2,64,1024]{2,1,0:T(8,128)(2,1)} %echoes.1, bf16[2,512]{1,0:T(2,128)(2,1)} %chirp.1, f32[64,64]{1,0:T(8,128)} %phase_in.1, s32[64,64]{1,0:T(8,128)} %shift_in.1, s32[2,2,8,32]{3,2,1,0:T(8,128)} %ktaps_in.1, s32[2,2,32]{2,1,0:T(2,128)} %mshift_in.1, f32[2,2,2,8,32]{4,3,2,1,0:T(8,128)} %kweights_in.1), custom_call_target="tpu_custom_call" | custom-call | tf_op jit(solution)/shard_map/pallas_call | solution.py:358
  28.5 1.6 %copy.9 = bf16[2,32,1024]{2,1,0:T(8,128)(2,1)} copy(bf16[2,32,1024]{2,1,0:T(8,128)(2,1)} %shard_map.73) | data formatting | bytes 262144

commit v3 on v1

--- a/solution.py
+++ b/solution.py
@@ -198,9 +198,20 @@
         at = pl.ds(tile * TILE, TILE)
         return sub_copy(pulses.at[0, :, :, at], pulses.at[1, :, :, at], 2 + tile)
 
+    def project(tile):
+        first = tile * TILE
+        pulse_copy(tile).wait_recv()
+        block = pulses[:, :, :, first : first + TILE].reshape(4 * local, TILE)
+        products[:, first : first + TILE] = jnp.dot(
+            select[...], block, preferred_element_type=F32
+        )
+
     arrived = 0
-    for tile in order:
+    for step, tile in enumerate(order):
         first = tile * TILE
+        if step == 2:
+            project(order[0])
+            project(order[1])
         if tile == 0:
             @pl.when(rng > 0)
             def _():
@@ -226,13 +237,8 @@
         pulses[0, 1, :, first : first + TILE] = jnp.where(keep, imag, 0.0).astype(BF16)
         pulse_copy(tile).start()
 
-    for tile in order:
-        first = tile * TILE
-        pulse_copy(tile).wait_recv()
-        block = pulses[:, :, :, first : first + TILE].reshape(4 * local, TILE)
-        products[:, first : first + TILE] = jnp.dot(
-            select[...], block, preferred_element_type=F32
-        )
+    for tile in order[2:] if len(order) > 2 else order:
+        project(tile)
 
     chunk = 16
     chunks = rows // chunk

time: 29.4 us -> 30.5 us (1.037)
  Pallas kernels: 27.7 us -> 28.8 us
    pallas_call x1, Pallas kernels: 27.7 us -> 28.8 us  [shards(): pl.pallas_call(functools.partial(image_kernel, n_rng, n_aper, levels, tup...]
where the time goes in v3:
time: 30.5 us; the launch traced here: 30.3 us
  Pallas kernels  28.8 us (94%)
  local copies, waits for them, and re-layouts  1.57 us (5%)
    pallas_call x1, Pallas kernels, shards(): pl.pallas_call(functools.partial(image_kernel, n_rng, n_aper, levels, tup...  28.8 us
    unnamed x1, local copies, waits for them, and re-layouts  1.57 us

profile of v3, /device:TPU:0, one launch (start us, length us, event | category | flops | bytes accessed | tf_op | source)
XLA Modules:
  0.0 30.3 jit_solution(7393555066033206079)
XLA Ops:
  0.0 28.8 %shard_map.73 = bf16[2,32,1024]{2,1,0:T(8,128)(2,1)} custom-call(bf16[2,64,1024]{2,1,0:T(8,128)(2,1)} %echoes.1, bf16[2,512]{1,0:T(2,128)(2,1)} %chirp.1, f32[64,64]{1,0:T(8,128)} %phase_in.1, s32[64,64]{1,0:T(8,128)} %shift_in.1, s32[2,2,8,32]{3,2,1,0:T(8,128)} %ktaps_in.1, s32[2,2,32]{2,1,0:T(2,128)} %mshift_in.1, f32[2,2,2,8,32]{4,3,2,1,0:T(8,128)} %kweights_in.1), custom_call_target="tpu_custom_call" | custom-call | tf_op jit(solution)/shard_map/pallas_call | solution.py:361
  28.8 1.6 %copy.9 = bf16[2,32,1024]{2,1,0:T(8,128)(2,1)} copy(bf16[2,32,1024]{2,1,0:T(8,128)(2,1)} %shard_map.73) | data formatting | bytes 262144

commit v4 on v1

--- a/solution.py
+++ b/solution.py
@@ -144,25 +144,6 @@
     for load in loads:
         load.wait()
 
-    beam_ids = lax.broadcasted_iota(jnp.int32, (beams, rows), 0)
-    for level in range(levels):
-        for child in range(2):
-            tap = ktaps[level, child]
-            real_w, imag_w = kweights[0, level, child], kweights[1, level, child]
-            tap2 = jnp.concatenate([tap, tap], axis=1)
-            upper_w = jnp.concatenate([real_w, imag_w], axis=1)
-            lower_w = jnp.concatenate([-imag_w, real_w], axis=1)
-            upper = jnp.zeros((beams, rows), F32)
-            lower = jnp.zeros((beams, rows), F32)
-            for t in range(tap.shape[0]):
-                match = beam_ids == tap2[t : t + 1, :]
-                upper = upper + jnp.where(match, upper_w[t : t + 1, :], 0.0)
-                lower = lower + jnp.where(match, lower_w[t : t + 1, :], 0.0)
-            kernels[level, child] = jnp.concatenate([upper, lower], axis=0).T.astype(BF16)
-            row = mshift[level, child : child + 1, :]
-            row2 = jnp.concatenate([row, row], axis=1) + REACH
-            row_shift[level, child] = jnp.broadcast_to(row2, (rows, rows)).T
-
     phase_copy.wait()
     shift_copy.wait()
 
@@ -271,6 +252,25 @@
             piece * chunk : (piece + 1) * chunk, :circle
         ].astype(BF16)
         level_copy(0, piece).start()
+
+    beam_ids = lax.broadcasted_iota(jnp.int32, (beams, rows), 0)
+    for level in range(levels):
+        for child in range(2):
+            tap = ktaps[level, child]
+            real_w, imag_w = kweights[0, level, child], kweights[1, level, child]
+            tap2 = jnp.concatenate([tap, tap], axis=1)
+            upper_w = jnp.concatenate([real_w, imag_w], axis=1)
+            lower_w = jnp.concatenate([-imag_w, real_w], axis=1)
+            upper = jnp.zeros((beams, rows), F32)
+            lower = jnp.zeros((beams, rows), F32)
+            for t in range(tap.shape[0]):
+                match = beam_ids == tap2[t : t + 1, :]
+                upper = upper + jnp.where(match, upper_w[t : t + 1, :], 0.0)
+                lower = lower + jnp.where(match, lower_w[t : t + 1, :], 0.0)
+            kernels[level, child] = jnp.concatenate([upper, lower], axis=0).T.astype(BF16)
+            row = mshift[level, child : child + 1, :]
+            row2 = jnp.concatenate([row, row], axis=1) + REACH
+            row_shift[level, child] = jnp.broadcast_to(row2, (rows, rows)).T
 
     def moved(level, child_of, source):
         matrix = jnp.where(child_of == 0, kernels[level, 0], kernels[level, 1])

time: 29.4 us -> 29.4 us (level)
  no operation moved by 1% of the time
where the time goes in v4:
time: 29.4 us; the launch traced here: 29.3 us
  Pallas kernels  27.7 us (94%)
  local copies, waits for them, and re-layouts  1.57 us (5%)
    pallas_call x1, Pallas kernels, shards(): pl.pallas_call(functools.partial(image_kernel, n_rng, n_aper, levels, tup...  27.7 us
    unnamed x1, local copies, waits for them, and re-layouts  1.57 us

profile of v4, /device:TPU:0, one launch (start us, length us, event | category | flops | bytes accessed | tf_op | source)
XLA Modules:
  0.0 29.3 jit_solution(1176425334573259132)
XLA Ops:
  0.0 27.7 %shard_map.73 = bf16[2,32,1024]{2,1,0:T(8,128)(2,1)} custom-call(bf16[2,64,1024]{2,1,0:T(8,128)(2,1)} %echoes.1, bf16[2,512]{1,0:T(2,128)(2,1)} %chirp.1, f32[64,64]{1,0:T(8,128)} %phase_in.1, s32[64,64]{1,0:T(8,128)} %shift_in.1, s32[2,2,8,32]{3,2,1,0:T(8,128)} %ktaps_in.1, s32[2,2,32]{2,1,0:T(2,128)} %mshift_in.1, f32[2,2,2,8,32]{4,3,2,1,0:T(8,128)} %kweights_in.1), custom_call_target="tpu_custom_call" | custom-call | tf_op jit(solution)/shard_map/pallas_call | solution.py:355
  27.7 1.6 %copy.9 = bf16[2,32,1024]{2,1,0:T(8,128)(2,1)} copy(bf16[2,32,1024]{2,1,0:T(8,128)(2,1)} %shard_map.73) | data formatting | bytes 262144
